TPU v7x, 32 devices: a whole 2x2x4 slice. The times are simulated.
32 devices in a mesh: seq: 4 (over y, core), fsdp: 8 (over z, x).
Axes of the slice: x: 2, y: 2, z: 4, core: 2. Of those that a mesh axis runs over, the one named last changes fastest.
Arguments:
- tokens: bfloat16 [8, 1536, 768], P('fsdp', 'seq'), may hold values from -6 to 6
- cotangent: bfloat16 [8, 1536, 768], P('fsdp', 'seq'), may hold values from -6 to 6
- expert_ids: int32 [8, 1536, 1], P('fsdp', 'seq'), may hold values from 0 to 7; in each aligned block of 384 rows (0 to 383, 384 to 767, ..., all dimensions but the last counted through in order) at most 64 rows name the same one
- bucket_ids: int32 [3071], replicated, may hold values from 0 to 31
- first_gain: bfloat16 [768], P('fsdp'), may hold values from 0.5 to 1.5
- query_weight: bfloat16 [768, 768], P('fsdp'), may hold values from -0.02734375 to 0.02734375
- key_weight: bfloat16 [768, 768], P('fsdp'), may hold values from -0.21875 to 0.21875
- value_weight: bfloat16 [768, 768], P('fsdp'), may hold values from -0.21875 to 0.21875
- output_weight: bfloat16 [768, 768], P('fsdp'), may hold values from -3 to 3
- bias_table: bfloat16 [12, 32], P('seq'), may hold values from -6 to 6
- second_gain: bfloat16 [768], P('fsdp'), may hold values from 0.5 to 1.5
- router_weight: bfloat16 [768, 8], P('fsdp'), may hold values from -0.15625 to 0.15625
- inner_weight: bfloat16 [8, 768, 3072], P('fsdp'), may hold values from -0.21875 to 0.21875
- outer_weight: bfloat16 [8, 3072, 768], P('fsdp'), may hold values from -0.875 to 0.875
Outputs:
- layer_out: bfloat16 [8, 1536, 768], P('fsdp', 'seq')
- tokens_grad: bfloat16 [8, 1536, 768], P('fsdp', 'seq')
- first_gain_grad: float32 [768], P(('seq', 'fsdp'))
- query_grad: float32 [768, 768], P('fsdp', 'seq')
- key_grad: float32 [768, 768], P('fsdp', 'seq')
- value_grad: float32 [768, 768], P('fsdp', 'seq')
- output_grad: float32 [768, 768], P(('seq', 'fsdp'))
- table_grad: float32 [12, 32], P('seq')
- second_gain_grad: float32 [768], P(('seq', 'fsdp'))
- router_grad: float32 [768, 8], P(('seq', 'fsdp'))
- inner_grad: float32 [8, 768, 3072], P('fsdp', None, 'seq')
- outer_grad: float32 [8, 3072, 768], P('fsdp', 'seq')
Inputs may be any that keep to these rules, and one draw needn't show every extreme that they name: `expert_ids`: within one block of 384 consecutive tokens of a sequence no expert is named more than 64 times; some expert reaches 64 in some block.
All inputs are finite; a program needn't handle non-finite values.
Results may differ from a plain program's by a relative error of at most 0.019.
Values may be sent and summed in bfloat16 or wider, within the bound.
No kernel may reach another device: no remote copies, remote signals or barrier semaphores. Data moves between devices by JAX's collectives and lax.ppermute only.
A program may use at most 192 MiB of HBM per device.

v0:
```python
import functools

import jax
import jax.numpy as jnp
from jax import lax
from jax.experimental import pallas as pl
from jax.experimental.pallas import tpu as pltpu
from jax.sharding import PartitionSpec as P

EPSILON = 1e-06
STRIP = 128
EXTRA = 8
VMEM_LIMIT = 56 * 1024 * 1024
NT = (((1,), (1,)), ((), ()))
NN = (((1,), (0,)), ((), ()))
LOW = jnp.bfloat16
WIDE = jnp.float32


def product(left, right, dims=NN):
    return lax.dot_general(left, right, dims, preferred_element_type=WIDE)


def flip(values):
    return values.astype(WIDE).T.astype(LOW)


def swap(values, axis, offset):
    count = lax.axis_size(axis)
    return lax.ppermute(values, axis, [(i, i ^ offset) for i in range(count)])


def cost(microseconds):
    return pl.CostEstimate(
        flops=int(microseconds * 1.15e9), bytes_accessed=1024, transcendentals=0
    )


def call(kernel, inputs, outputs, scratch=(), where=None, time=2):
    specs = [pl.BlockSpec(memory_space=pltpu.VMEM)] * len(inputs)
    operands = list(inputs)
    if where is not None:
        specs = [pl.BlockSpec(memory_space=pltpu.SMEM)] + specs
        operands = [where] + operands
    return pl.pallas_call(
        kernel,
        in_specs=specs,
        out_specs=[pl.BlockSpec(memory_space=pltpu.VMEM)] * len(outputs),
        out_shape=[jax.ShapeDtypeStruct(shape, dtype) for shape, dtype in outputs],
        scratch_shapes=list(scratch),
        compiler_params=pltpu.CompilerParams(vmem_limit_bytes=VMEM_LIMIT),
        cost_estimate=cost(time),
    )(*operands)


def strip_kernel(table_ref, bucket_ref, strip_ref):
    heads = strip_ref.shape[0]
    span = bucket_ref.shape[1]
    ids = lax.broadcasted_iota(jnp.int32, (table_ref.shape[1], span), 0)
    hot = jnp.where(ids == bucket_ref[...], 1.0, 0.0).astype(LOW)
    relative = product(table_ref[...], hot)
    for head in range(heads):
        wide = jnp.broadcast_to(relative[head : head + 1, :], (STRIP, span))
        strip_ref[head] = pltpu.roll(wide, span - STRIP + 1, 1, stride=1, stride_axis=0)


def forward_kernel(where_ref, *refs, heads, size, seq_count, weight_parts):
    token_refs = refs[:seq_count]
    weight_refs = refs[seq_count : seq_count + weight_parts]
    strip_ref = refs[seq_count + weight_parts]
    (
        normed_ref, q_ref, k_ref, v_ref, wq_ref, wk_ref, wv_ref, extra_ref, o32_ref, share_ref,
        weights_ref,
    ) = refs[seq_count + weight_parts + 1 : seq_count + weight_parts + 12]
    mixed_refs = refs[seq_count + weight_parts + 12 : -2]
    joined_ref, vext_ref = refs[-2:]
    length, width = k_ref.shape
    rows = length // seq_count
    step = pl.program_id(0)
    me = where_ref[0]
    owner_row = where_ref[1]

    @pl.when(step == 0)
    def _():
        if weight_parts == 1:
            joined_ref[...] = weight_refs[0][...]
        else:
            share = weight_refs[0].shape[0]
            offsets = [2 * part for part in range(weight_parts - 2)] + [1]
            for part, offset in enumerate(offsets):
                place = pl.multiple_of((owner_row ^ offset) * share, 16)
                joined_ref[pl.ds(place, share), :] = weight_refs[part][...]
            for part in range(1, weight_parts - 2):
                place = pl.multiple_of((owner_row ^ (2 * part + 1)) * share, 16)
                joined_ref[pl.ds(place, share), :] = weight_refs[-1][
                    (part - 1) * share : part * share, :
                ]
        extra_ref[...] = joined_ref[:, :128].astype(WIDE).T
        joined = joined_ref[...]
        wq_ref[...] = joined[:, 128 : 128 + width]
        wk_ref[...] = joined[:, 128 + width : 128 + 2 * width]
        wv_ref[...] = joined[:, 128 + 2 * width : 128 + 3 * width]
        gain = extra_ref[0:1, :]
        for part in range(seq_count):
            place = pl.ds(pl.multiple_of((me ^ part) * rows, rows), rows)
            inputs = token_refs[part][...].astype(WIDE)
            factor = lax.rsqrt(jnp.mean(inputs * inputs, axis=1, keepdims=True) + EPSILON)
            normed = (inputs * factor * gain).astype(LOW)
            normed_ref[place, :] = normed
            q_ref[place, :] = product(normed, wq_ref[...]).astype(LOW)
            k_ref[place, :] = product(normed, wk_ref[...]).astype(LOW)
            values = product(normed, wv_ref[...]).astype(LOW)
            v_ref[place, :] = values
            vext_ref[place, :width] = values
        vext_ref[:, width:] = jnp.ones((length, 256 - width), LOW)

    for part in range(rows // STRIP):
        block = (me ^ step) * (rows // STRIP) + part
        start = pl.multiple_of((length // STRIP - 1 - block) * STRIP, STRIP)
        q = q_ref[pl.ds(pl.multiple_of(block * STRIP, STRIP), STRIP), :]
        owner = lax.broadcasted_iota(jnp.int32, (STRIP, width), 1) // size
        lanes = lax.broadcasted_iota(jnp.int32, (STRIP, 128), 1)
        total = jnp.zeros((STRIP, width), WIDE)
        shares = jnp.zeros((STRIP, 128), WIDE)
        place = slice(part * STRIP, (part + 1) * STRIP)
        for head in range(heads):
            scores = product(jnp.where(owner == head, q, jnp.zeros_like(q)), k_ref[...], NT)
            scores = scores + strip_ref[head, :, pl.ds(start, length)]
            high = jnp.max(scores, axis=1, keepdims=True)
            weights = jnp.exp(scores - high).astype(LOW)
            mixed = product(weights, vext_ref[...])
            weights_ref[head, place, :] = weights
            share = 1.0 / mixed[:, width : width + 1]
            total = jnp.where(owner == head, mixed[:, :width] * share, total)
            shares = jnp.where(lanes == head, share, shares)
        o32_ref[place, :] = total
        share_ref[place, :] = shares
        for offset in range(seq_count):

            @pl.when(step == offset)
            def _():
                mixed_refs[offset][place, :] = total.astype(LOW)


def forward_attention(where, token_parts, weight_parts, strip, size):
    seq_count = len(token_parts)
    rows, features = token_parts[0].shape
    length = rows * seq_count
    columns = weight_parts[0].shape[1]
    width = (columns - 128) // 3
    heads = width // size
    full = lambda *shape: pl.BlockSpec(shape, lambda i, w: (0,) * len(shape))
    block = lambda w: pl.BlockSpec((rows, w), lambda i, w_: (i, 0))
    shaped = jax.ShapeDtypeStruct
    results = pl.pallas_call(
        functools.partial(
            forward_kernel,
            heads=heads,
            size=size,
            seq_count=seq_count,
            weight_parts=len(weight_parts),
        ),
        grid_spec=pltpu.PrefetchScalarGridSpec(
            num_scalar_prefetch=1,
            grid=(seq_count,),
            in_specs=[full(*a.shape) for a in (*token_parts, *weight_parts, strip)],
            out_specs=[full(length, features)]
            + [full(length, width)] * 3
            + [full(features, width)] * 3
            + [full(128, features), block(width), block(128)]
            + [pl.BlockSpec((heads, rows, length), lambda i, w: (0, i, 0))]
            + [full(rows, width)] * seq_count,
            scratch_shapes=[pltpu.VMEM((features, columns), LOW), pltpu.VMEM((length, 256), LOW)],
        ),
        out_shape=[shaped((length, features), LOW)]
        + [shaped((length, width), LOW)] * 3
        + [shaped((features, width), LOW)] * 3
        + [
            shaped((128, features), WIDE),
            shaped((length, width), WIDE),
            shaped((length, 128), WIDE),
            shaped((heads, length, length), LOW),
        ]
        + [shaped((rows, width), LOW)] * seq_count,
        compiler_params=pltpu.CompilerParams(vmem_limit_bytes=VMEM_LIMIT),
        cost_estimate=cost(35),
    )(where, *token_parts, *weight_parts, strip)
    return results[:11], results[11:]


def place_rows(where_ref, joined_ref, part_refs):
    part_rows = joined_ref.shape[0] // len(part_refs)
    for part, part_ref in enumerate(part_refs):
        place = pl.multiple_of((where_ref[1] ^ part) * part_rows, 16) if len(part_refs) > 1 else 0
        joined_ref[pl.ds(place, part_rows), :] = part_ref[...]


def send_kernel(where_ref, *refs, seq_count, weight_parts, experts, capacity):
    mixed_refs = refs[:seq_count]
    weight_refs = refs[seq_count : seq_count + weight_parts]
    tokens_ref, cotangent_ref, ids_ref, extra_ref = refs[
        seq_count + weight_parts : seq_count + weight_parts + 4
    ]
    rest = refs[seq_count + weight_parts + 4 :]
    hidden_ref, normed_ref, notes_ref = rest[:3]
    both_ref, joined_ref = rest[3:]
    rows = tokens_ref.shape[0]
    width = mixed_refs[0].shape[1]
    place_rows(where_ref, joined_ref, weight_refs)
    hidden = tokens_ref[...].astype(WIDE)
    for part in range(seq_count):
        place = pl.multiple_of((where_ref[0] ^ part) * width, 64)
        hidden = hidden + product(mixed_refs[part][...], joined_ref[pl.ds(place, width), :])
    hidden_ref[...] = hidden
    factor = lax.rsqrt(jnp.mean(hidden * hidden, axis=1, keepdims=True) + EPSILON)
    normed = (hidden * factor * extra_ref[1:2, :]).astype(LOW)
    normed_ref[...] = normed
    logits = product(normed, extra_ref[...].astype(LOW), NT)
    lanes = lax.broadcasted_iota(jnp.int32, (rows, 128), 1)
    valid = (lanes >= EXTRA) & (lanes < EXTRA + experts)
    logits = jnp.where(valid, logits, -jnp.inf)
    powers = jnp.exp(logits - jnp.max(logits, axis=1, keepdims=True))
    probs = powers / jnp.sum(powers, axis=1, keepdims=True)
    ids = ids_ref[...]
    hot = lanes == ids + EXTRA
    gate = jnp.sum(jnp.where(hot, probs, 0.0), axis=1, keepdims=True)
    earlier_rows = lax.broadcasted_iota(jnp.int32, (rows, rows), 1) < lax.broadcasted_iota(
        jnp.int32, (rows, rows), 0
    )
    earlier = product(
        jnp.where(earlier_rows, 1.0, 0.0).astype(LOW), jnp.where(hot, 1.0, 0.0).astype(LOW)
    )
    slot = jnp.sum(jnp.where(hot, earlier, 0.0), axis=1, keepdims=True)
    placement = (ids * (2 * capacity)).astype(WIDE) + slot
    notes = jnp.where(lanes == 0, gate, probs)
    notes = jnp.where(lanes == 1, placement, notes)
    notes = jnp.where(lanes == 2, factor, notes)
    notes = jnp.where(lanes == 3, (ids + EXTRA).astype(WIDE), notes)
    notes_ref[...] = notes
    placement_row = notes.T[1:2, :].astype(jnp.int32)
    slot_ids = lax.broadcasted_iota(jnp.int32, (2 * experts * capacity, rows), 0)
    spread = jnp.concatenate(
        [
            jnp.where(slot_ids == placement_row, 1.0, 0.0).astype(LOW),
            jnp.where(slot_ids == placement_row + capacity, 1.0, 0.0).astype(LOW),
        ],
        axis=1,
    )
    picked_grad = (gate * cotangent_ref[...].astype(WIDE)).astype(LOW)
    both_ref[...] = product(spread, jnp.concatenate([normed, picked_grad], axis=0)).astype(LOW)


def expert_kernel(
    both_ref, inner_ref, outer_ref, active_ref, pre_grad_ref, slots_ref, grads_ref, back_ref,
    out_ref, slots_grad_ref, *, sources,
):
    step = pl.program_id(0)
    slot_count, features = slots_ref.shape
    apart = (sources, 2, slot_count // sources, features)

    @pl.when(step == 0)
    def _():
        both = both_ref[...].astype(WIDE).reshape(apart)
        slots_ref[...] = both[:, 0].reshape(slot_count, features).astype(LOW)
        grads_ref[...] = both[:, 1].reshape(slot_count, features).astype(LOW)
        out_ref[...] = jnp.zeros_like(out_ref)
        slots_grad_ref[...] = jnp.zeros_like(slots_grad_ref)

    pre = product(slots_ref[...], inner_ref[...])
    active_grad = product(grads_ref[...], outer_ref[...], NT)
    scale = 0.7978845608028654
    square = pre * pre
    bent = jnp.tanh(pre * (scale + scale * 0.044715 * square))
    half = 0.5 + 0.5 * bent
    active = (pre * half).astype(LOW)
    slope = half + 0.5 * pre * (1.0 - bent * bent) * (scale + 3.0 * scale * 0.044715 * square)
    pre_grad = (active_grad * slope).astype(LOW)
    active_ref[...] = active
    pre_grad_ref[...] = pre_grad
    out_ref[...] += product(active, outer_ref[...])
    slots_grad_ref[...] += product(pre_grad, inner_ref[...], NT)

    @pl.when(step == pl.num_programs(0) - 1)
    def _():
        each = (sources, 1, slot_count // sources, features)
        back = jnp.concatenate(
            [out_ref[...].reshape(each), slots_grad_ref[...].reshape(each)], axis=1
        )
        back_ref[...] = back.reshape(2 * slot_count, features).astype(LOW)


def expert_step(both, inner, outer, sources, chunk=512):
    slot_count = both.shape[0] // 2
    features, units = inner.shape
    full = lambda *shape: pl.BlockSpec(shape, lambda i: (0,) * len(shape))
    across = pl.BlockSpec((slot_count, chunk), lambda i: (0, i))
    shaped = jax.ShapeDtypeStruct
    return pl.pallas_call(
        functools.partial(expert_kernel, sources=sources),
        grid=(units // chunk,),
        in_specs=[
            full(2 * slot_count, features),
            pl.BlockSpec((features, chunk), lambda i: (0, i)),
            pl.BlockSpec((chunk, features), lambda i: (i, 0)),
        ],
        out_specs=[
            across,
            across,
            full(slot_count, features),
            full(slot_count, features),
            full(2 * slot_count, features),
        ],
        out_shape=[
            shaped((slot_count, units), LOW),
            shaped((slot_count, units), LOW),
            shaped((slot_count, features), LOW),
            shaped((slot_count, features), LOW),
            shaped((2 * slot_count, features), LOW),
        ],
        scratch_shapes=[
            pltpu.VMEM((slot_count, features), WIDE),
            pltpu.VMEM((slot_count, features), WIDE),
        ],
        compiler_params=pltpu.CompilerParams(vmem_limit_bytes=VMEM_LIMIT),
        cost_estimate=cost(24),
    )(both, inner, outer)


def return_kernel(where_ref, *refs, seq_count, weight_parts, experts, capacity):
    mixed_refs = refs[:seq_count]
    weight_refs = refs[seq_count : seq_count + weight_parts]
    refs = refs[seq_count + weight_parts :]
    back_ref = refs[0]
    refs = refs[1:]
    hidden_ref, normed_ref, notes_ref, cotangent_ref, extra_ref = refs[:5]
    layer_ref, hidden_grad_ref, output_grad_ref = refs[5:8]
    mixed_grad_refs = refs[8 : 8 + seq_count]
    joined_ref = refs[-1]
    rows, features = hidden_ref.shape
    width = mixed_refs[0].shape[1]
    place_rows(where_ref, joined_ref, weight_refs)
    notes = notes_ref[...]
    gate = notes[:, 0:1]
    placement = notes[:, 1:2].astype(jnp.int32)
    factor = notes[:, 2:3]
    own_lane = notes[:, 3:4].astype(jnp.int32)
    hidden = hidden_ref[...]
    cotangent = cotangent_ref[...].astype(WIDE)
    slot_ids = lax.broadcasted_iota(jnp.int32, (rows, back_ref.shape[0]), 1)
    picked = product(jnp.where(slot_ids == placement, 1.0, 0.0).astype(LOW), back_ref[...])
    layer_ref[...] = (hidden + gate * picked).astype(LOW)
    gate_grad = jnp.sum(cotangent * picked, axis=1, keepdims=True)
    lanes = lax.broadcasted_iota(jnp.int32, (rows, 128), 1)
    valid = (lanes >= EXTRA) & (lanes < EXTRA + experts)
    probs = jnp.where(valid, notes, 0.0)
    prob_grad = jnp.where(lanes == own_lane, gate_grad, 0.0)
    logit_grad = probs * (prob_grad - gate * gate_grad)
    logit_grad_low = logit_grad.astype(LOW)
    normed_grad = product(
        jnp.where(slot_ids == placement + capacity, 1.0, 0.0).astype(LOW), back_ref[...]
    )
    normed_grad = normed_grad + product(logit_grad_low, extra_ref[...].astype(LOW))
    scaled = normed_grad * hidden
    gain = extra_ref[1:2, :]
    center = jnp.mean(scaled * gain, axis=1, keepdims=True)
    hidden_grad = cotangent + factor * (gain * normed_grad) - hidden * (
        factor * factor * factor * center
    )
    hidden_grad_ref[...] = hidden_grad
    small = product(logit_grad.T.astype(LOW), normed_ref[...])
    gain_grad = jnp.sum(scaled * factor, axis=0, keepdims=True)
    small = jnp.where(lax.broadcasted_iota(jnp.int32, small.shape, 0) == 1, gain_grad, small)
    output_grad_ref[:, features:] = small.T.astype(LOW)
    branch = hidden_grad.astype(LOW)
    for part in range(seq_count):
        place = pl.ds(pl.multiple_of((where_ref[0] ^ part) * width, 64), width)
        mixed_grad_refs[part][...] = product(branch, joined_ref[place, :], NT).astype(LOW)
        output_grad_ref[place, :features] = product(flip(mixed_refs[part][...]), branch).astype(
            LOW
        )


def three_parts(value):
    first = value.astype(LOW)
    rest = value - first.astype(WIDE)
    second = rest.astype(LOW)
    third = (rest - second.astype(WIDE)).astype(LOW)
    return first, second, third


def attend_back_kernel(where_ref, *refs, heads, size, seq_count):
    grad_refs = refs[:seq_count]
    q_ref, k_ref, v_ref, o32_ref, share_ref, weights_ref = refs[seq_count : seq_count + 6]
    dq_ref, dkt_ref, dvt_ref, strip_grad_ref = refs[seq_count + 6 : seq_count + 10]
    vext_ref, grad_ref = refs[seq_count + 10 :]
    length, width = k_ref.shape
    rows = length // seq_count
    step = pl.program_id(0)
    me = where_ref[0]

    @pl.when(step == 0)
    def _():
        vext_ref[:, :width] = v_ref[...]
        vext_ref[:, width:] = jnp.ones((length, 256 - width), LOW)
        dkt_ref[...] = jnp.zeros_like(dkt_ref)
        dvt_ref[...] = jnp.zeros_like(dvt_ref)
        strip_grad_ref[...] = jnp.zeros_like(strip_grad_ref)

    for offset in range(seq_count):

        @pl.when(step == offset)
        def _():
            grad_ref[...] = grad_refs[offset][...]

    for part in range(rows // STRIP):
        block = (me ^ step) * (rows // STRIP) + part
        start = pl.multiple_of((length // STRIP - 1 - block) * STRIP, STRIP)
        token_rows = pl.ds(pl.multiple_of(block * STRIP, STRIP), STRIP)
        own_rows = slice(part * STRIP, (part + 1) * STRIP)
        owner = lax.broadcasted_iota(jnp.int32, (STRIP, width), 1) // size
        tail = lax.broadcasted_iota(jnp.int32, (STRIP, 256 - width), 1)
        share = jnp.zeros((STRIP, width), WIDE)
        for head in range(heads):
            share = jnp.where(owner == head, share_ref[own_rows, head : head + 1], share)
        scaled = grad_ref[own_rows, :].astype(WIDE) * share
        mixed_product = scaled * o32_ref[own_rows, :]
        grad_flipped = scaled.T.astype(LOW)
        scaled = scaled.astype(LOW)
        q_flipped = flip(q_ref[token_rows, :])
        total = jnp.zeros((STRIP, width), WIDE)
        for head in range(heads):
            mine = owner == head
            head_rows = slice(head * size, (head + 1) * size)
            delta = jnp.sum(jnp.where(mine, mixed_product, 0.0), axis=1, keepdims=True)
            first, second, third = three_parts(-delta)
            added = jnp.where(tail == 2, third, jnp.zeros_like(third))
            added = jnp.where(tail == 0, first, jnp.where(tail == 1, second, added))
            own_grad = jnp.concatenate([jnp.where(mine, scaled, jnp.zeros_like(scaled)), added], 1)
            weights = weights_ref[head, own_rows, :]
            score_grad = weights.astype(WIDE) * product(own_grad, vext_ref[...], NT)
            strip_grad_ref[head, :, pl.ds(start, length)] += score_grad
            score_grad = score_grad.astype(LOW)
            dvt_ref[head_rows, :] += product(grad_flipped[head_rows, :], weights)
            dkt_ref[head_rows, :] += product(q_flipped[head_rows, :], score_grad)
            total = jnp.where(mine, product(score_grad, k_ref[...]), total)
        dq_ref[token_rows, :] = total.astype(LOW)


def backward_attention(where, grad_parts, q, k, v, o32, shares, attention, strip_shape):
    seq_count = len(grad_parts)
    length, width = q.shape
    rows = length // seq_count
    heads = attention.shape[0]
    full = lambda *shape: pl.BlockSpec(shape, lambda i, w: (0,) * len(shape))
    block = lambda w: pl.BlockSpec((rows, w), lambda i, w_: (i, 0))
    shaped = jax.ShapeDtypeStruct
    return pl.pallas_call(
        functools.partial(
            attend_back_kernel, heads=heads, size=width // heads, seq_count=seq_count
        ),
        grid_spec=pltpu.PrefetchScalarGridSpec(
            num_scalar_prefetch=1,
            grid=(seq_count,),
            in_specs=[full(rows, width)] * seq_count
            + [full(length, width)] * 3
            + [block(width), block(128)]
            + [pl.BlockSpec((heads, rows, length), lambda i, w: (0, i, 0))],
            out_specs=[
                full(length, width),
                full(width, length),
                full(width, length),
                full(*strip_shape),
            ],
            scratch_shapes=[pltpu.VMEM((length, 256), LOW), pltpu.VMEM((rows, width), LOW)],
        ),
        out_shape=[
            shaped((length, width), LOW),
            shaped((width, length), WIDE),
            shaped((width, length), WIDE),
            shaped(strip_shape, WIDE),
        ],
        compiler_params=pltpu.CompilerParams(vmem_limit_bytes=VMEM_LIMIT),
        cost_estimate=cost(32),
    )(where, *grad_parts, q, k, v, o32, shares, attention)


def weight_kernel(normed_ref, dq_ref, dkt_ref, dvt_ref, out_ref):
    flipped = jnp.concatenate(
        [flip(dq_ref[...]), dkt_ref[...].astype(LOW), dvt_ref[...].astype(LOW)], axis=0
    )
    out_ref[...] = product(flipped, normed_ref[...]).T.astype(LOW)


def row_kernel(
    where_ref, normed_ref, dq_ref, dkt_ref, dvt_ref, wq_ref, wk_ref, wv_ref, extra_ref, *refs,
    seq_count,
):
    row_refs = refs[:seq_count]
    gain_ref, dk_ref, dv_ref = refs[seq_count:]
    length, width = dq_ref.shape
    rows = length // seq_count
    dk_ref[...] = dkt_ref[...].T.astype(LOW)
    dv_ref[...] = dvt_ref[...].T.astype(LOW)
    gain_sum = jnp.zeros((1, normed_ref.shape[1]), WIDE)
    for part in range(seq_count):
        place = pl.ds(pl.multiple_of((where_ref[0] ^ part) * rows, rows), rows)
        row_grad = product(dq_ref[place, :], wq_ref[...], NT)
        row_grad = row_grad + product(dk_ref[place, :], wk_ref[...], NT)
        row_grad = row_grad + product(dv_ref[place, :], wv_ref[...], NT)
        row_refs[part][...] = row_grad.astype(LOW)
        gain_sum = gain_sum + jnp.sum(
            row_grad * normed_ref[place, :].astype(WIDE), axis=0, keepdims=True
        )
    gain_ref[...] = gain_sum / extra_ref[0:1, :]


def table_kernel(strip_grad_ref, bucket_ref, out_ref, *, bucket_count):
    heads, _, span = strip_grad_ref.shape
    sums = []
    for head in range(heads):
        folded = strip_grad_ref[head]
        half = STRIP // 2
        while half >= 1:
            folded = pltpu.roll(folded[:half], half, 1) + folded[half:]
            half //= 2
        sums.append(folded)
    diagonals = jnp.concatenate(sums + [jnp.zeros((8 - heads, span), WIDE)], axis=0)
    ids = lax.broadcasted_iota(jnp.int32, (bucket_count, span), 0)
    hot = jnp.where(ids == bucket_ref[...], 1.0, 0.0)
    out_ref[...] = lax.dot_general(
        diagonals, hot, NT, preferred_element_type=WIDE, precision=lax.Precision.HIGHEST
    )


def finish_kernel(*refs, seq_count):
    row_refs = refs[:seq_count]
    tokens_ref, hidden_grad_ref, extra_ref, out_ref = refs[seq_count:]
    normed_grad = row_refs[0][...].astype(WIDE)
    for part in range(1, seq_count):
        normed_grad = normed_grad + row_refs[part][...].astype(WIDE)
    inputs = tokens_ref[...].astype(WIDE)
    factor = lax.rsqrt(jnp.mean(inputs * inputs, axis=1, keepdims=True) + EPSILON)
    scaled = normed_grad * extra_ref[0:1, :]
    center = jnp.mean(scaled * inputs, axis=1, keepdims=True)
    out_ref[...] = (
        hidden_grad_ref[...] + factor * scaled - inputs * (factor * factor * factor * center)
    ).astype(LOW)


def sum_kernel(parts_ref, *out_refs):
    total = parts_ref[0].astype(WIDE)
    for part in range(1, parts_ref.shape[0]):
        total = total + parts_ref[part].astype(WIDE)
    start = 0
    for out_ref in out_refs:
        width = out_ref.shape[1]
        out_ref[...] = total[:, start : start + width]
        start += width


def on_device(
    tokens,
    cotangent,
    expert_ids,
    bucket_ids,
    first_gain,
    query_weight,
    key_weight,
    value_weight,
    output_weight,
    bias_table,
    second_gain,
    router_weight,
    inner_weight,
    outer_weight,
):
    seq_count = lax.axis_size("seq")
    owner_count = lax.axis_size("fsdp")
    pairwise = owner_count <= 8
    me = lax.axis_index("seq").astype(jnp.int32)
    owner = lax.axis_index("fsdp").astype(jnp.int32)
    rows, features = tokens.shape[1:]
    experts = router_weight.shape[1]
    capacity = max(2, 4 * rows // (3 * experts))
    slot_count = experts * capacity
    heads, bucket_count = bias_table.shape
    width = features // seq_count
    size = width // heads
    where = jnp.stack([me, owner, jnp.zeros_like(owner)])
    weight_parts = owner_count if pairwise else 1

    def exchange(values):
        split = values.reshape(owner_count, -1, values.shape[1])
        return lax.all_to_all(split, "fsdp", 0, 0, tiled=True)

    def exchange_seq(parts):
        return [parts[0]] + [swap(parts[s], "seq", s) for s in range(1, seq_count)]

    token_block = tokens[0]
    grad_block = cotangent[0]
    columns = lambda weight: lax.dynamic_slice_in_dim(weight, me * width, width, 1)
    extras = jnp.concatenate(
        [
            first_gain[:, None],
            second_gain[:, None],
            jnp.zeros((first_gain.shape[0], EXTRA - 2), LOW),
            router_weight,
            jnp.zeros((first_gain.shape[0], 128 - EXTRA - experts), LOW),
        ],
        axis=1,
    )
    bundle = jnp.concatenate(
        [extras, columns(query_weight), columns(key_weight), columns(value_weight)], axis=1
    )
    bucket_row = jnp.pad(bucket_ids, (0, 1))[None]
    padded_table = jnp.pad(bias_table, ((0, 16 - heads), (0, 0)))
    span = bucket_row.shape[1]
    weights = [bundle]
    if pairwise:
        weights += [swap(bundle, "fsdp", s) for s in range(2, owner_count, 2)]
        weights.append(swap(bundle, "fsdp", 1))
    far_tokens = swap(token_block, "seq", 2)
    near_tokens = swap(token_block, "seq", 1)
    (strip,) = call(
        strip_kernel, [padded_table, bucket_row], [((heads, STRIP, span), WIDE)], time=4
    )
    if pairwise:
        weights.append(swap(jnp.concatenate(weights[1:-1], axis=0), "fsdp", 1))
    else:
        weights = [lax.all_gather(bundle, "fsdp", axis=0, tiled=True)]
    token_parts = [token_block, near_tokens, far_tokens, swap(far_tokens, "seq", 1)]
    held, _, _ = lax.optimization_barrier((output_weight, weights, token_parts))
    output_weights = [lax.all_gather(held, "fsdp", axis=0, tiled=True)]

    kept, mixed_parts = forward_attention(where, token_parts, weights, strip, size)
    normed, q, k, v, wq, wk, wv, extra, o32, shares, attention = kept
    mixed_parts = exchange_seq(mixed_parts)

    hidden, normed_two, notes, both_slots = call(
        functools.partial(
            send_kernel,
            seq_count=seq_count,
            weight_parts=1,
            experts=experts,
            capacity=capacity,
        ),
        [*mixed_parts, *output_weights, token_block, grad_block, expert_ids[0], extra],
        [
            ((rows, features), WIDE),
            ((rows, features), LOW),
            ((rows, 128), WIDE),
            ((2 * slot_count, features), LOW),
        ],
        [pltpu.VMEM((features, features), LOW)],
        where,
        time=6,
    )
    received_both = exchange(both_slots).reshape(2 * slot_count, features)
    active, pre_grad, received, received_grad, back = expert_step(
        received_both, inner_weight[0], outer_weight[0], owner_count
    )
    returned = exchange(back).reshape(2 * slot_count, features)
    transposed = (((0,), (0,)), ((), ()))
    inner_term = product(received, pre_grad, transposed).astype(LOW)
    outer_term = product(active, received_grad, transposed).astype(LOW)
    inner_grad = lax.psum_scatter(inner_term, "seq", scatter_dimension=1, tiled=True)
    outer_grad = lax.psum_scatter(outer_term, "seq", scatter_dimension=0, tiled=True)

    results = call(
        functools.partial(
            return_kernel,
            seq_count=seq_count,
            weight_parts=1,
            experts=experts,
            capacity=capacity,
        ),
        [
            *mixed_parts,
            *output_weights,
            returned,
            hidden,
            normed_two,
            notes,
            grad_block,
            extra,
        ],
        [
            ((rows, features), LOW),
            ((rows, features), WIDE),
            ((features, features + 128), LOW),
        ]
        + [((rows, width), LOW)] * seq_count,
        [pltpu.VMEM((features, features), LOW)],
        where,
        time=8,
    )
    layer_out, hidden_grad, output_term = results[:3]
    mixed_grads = exchange_seq(results[3:])
    both = ("seq", "fsdp")
    device_count = seq_count * owner_count
    share = features // device_count
    held, _ = lax.optimization_barrier((output_term, mixed_grads))
    output_terms = lax.all_to_all(
        held.reshape(device_count, share, features + 128), both, 0, 0, tiled=True
    )
    dq, dkt, dvt, strip_grad = backward_attention(
        where, mixed_grads, q, k, v, o32, shares, attention, strip.shape
    )
    dq, output_terms = lax.optimization_barrier((dq, output_terms))
    (weight_terms,) = call(
        weight_kernel, [normed, dq, dkt, dvt], [((features, 3 * width), LOW)], time=6
    )
    held_dq, weight_terms = lax.optimization_barrier((dq, weight_terms))
    weight_terms = exchange(weight_terms)
    results = call(
        functools.partial(row_kernel, seq_count=seq_count),
        [normed, held_dq, dkt, dvt, wq, wk, wv, extra],
        [((rows, features), LOW)] * seq_count + [((1, features), WIDE)],
        [
            pltpu.VMEM((rows * seq_count, width), LOW),
            pltpu.VMEM((rows * seq_count, width), LOW),
        ],
        where,
        time=6,
    )
    row_grads, first_sum = results[:seq_count], results[seq_count]
    near, far = swap(row_grads[1], "seq", 1), swap(row_grads[3], "seq", 1)
    passed = (row_grads[2].astype(WIDE) + far.astype(WIDE)).astype(LOW)
    row_grads = [row_grads[0], near, swap(passed, "seq", 2)]
    (table_sums,) = call(
        functools.partial(table_kernel, bucket_count=bucket_count),
        [lax.optimization_barrier((strip_grad, first_sum))[0], bucket_row],
        [((8, bucket_count), WIDE)],
        time=5,
    )
    small = jnp.concatenate([first_sum.reshape(-1), table_sums[:heads].reshape(-1)])
    offset = 1
    while offset < owner_count:
        small = small + swap(small, "fsdp", offset)
        offset *= 2
    table_grad = small[features:].reshape(heads, bucket_count)
    small = small[:features]
    offset = 1
    while offset < seq_count:
        small = small + swap(small, "seq", offset)
        offset *= 2
    output_grad, others = call(
        sum_kernel, [output_terms], [((share, features), WIDE), ((share, 128), WIDE)]
    )
    (tokens_grad,) = call(
        functools.partial(finish_kernel, seq_count=len(row_grads)),
        [*row_grads, token_block, hidden_grad, extra],
        [((rows, features), LOW)],
        time=3,
    )
    first_grad = lax.dynamic_slice_in_dim(small, (me * owner_count + owner) * share, share, 0)
    weight_terms, inner_grad, outer_grad = lax.optimization_barrier(
        (weight_terms, inner_grad.astype(WIDE)[None], outer_grad.astype(WIDE)[None])
    )
    query_grad, key_grad, value_grad = call(
        sum_kernel, [weight_terms], [((features // owner_count, width), WIDE)] * 3
    )
    return (
        layer_out[None],
        tokens_grad[None],
        first_grad,
        query_grad,
        key_grad,
        value_grad,
        output_grad,
        table_grad,
        others[:, 1],
        others[:, EXTRA : EXTRA + experts],
        inner_grad,
        outer_grad,
    )


def solution(mesh):
    return jax.shard_map(
        on_device,
        mesh=mesh,
        in_specs=(
            P("fsdp", "seq", None),
            P("fsdp", "seq", None),
            P("fsdp", "seq", None),
            P(),
            P("fsdp"),
            P("fsdp", None),
            P("fsdp", None),
            P("fsdp", None),
            P("fsdp", None),
            P("seq", None),
            P("fsdp"),
            P("fsdp", None),
            P("fsdp", None, None),
            P("fsdp", None, None),
        ),
        out_specs=(
            P("fsdp", "seq", None),
            P("fsdp", "seq", None),
            P(("seq", "fsdp")),
            P("fsdp", "seq"),
            P("fsdp", "seq"),
            P("fsdp", "seq"),
            P(("seq", "fsdp"), None),
            P("seq", None),
            P(("seq", "fsdp")),
            P(("seq", "fsdp"), None),
            P("fsdp", None, "seq"),
            P("fsdp", "seq", None),
        ),
        check_vma=False,
    )
```

profile of v0, /device:TPU:0, one launch (start us, length us, event | category | flops | bytes accessed | tf_op | source)
XLA Modules:
  0.0 323.6 jit_solution(15802086810300315568)
XLA Ops:
  7.2 3.0 collective-permute-start.1
  23.8 5.6 %collective-permute-done.4.refs_6_ = bf16[96,704]{1,0:T(8,128)(2,1)S(1)} collective-permute-done((bf16[96,704]{1,0:T(8,128)(2,1)S(1)}, bf16[96,704]{1,0:T(8,128)(2,1)S(1)}, u32[]{:S(2)}, u32[]{:S(2)}) %collective-permute-start.4) | collective-permute-done | bytes 135200 | tf_op jit(solution)/shard_map/ppermute | solution.py:30
  31.0 4.3 %shard_map.229.refs_10_ = f32[3,128,3072]{2,1,0:T(8,128)} custom-call(bf16[16,32]{1,0:T(8,128)(2,1)} %pad.8.table_ref, s32[1,3072]{1,0:T(1,128)} %bitcast.35), custom_call_target="tpu_custom_call" | custom-call | flops 4600000000 | bytes 1024 | tf_op jit(solution)/shard_map/pallas_call | solution.py:45
  39.7 36.3 %shard_map.230 = (bf16[1536,768]{1,0:T(8,128)(2,1)}, bf16[1536,192]{1,0:T(8,128)(2,1)}, bf16[1536,192]{1,0:T(8,128)(2,1)}, bf16[1536,192]{1,0:T(8,128)(2,1)}, bf...) custom-call(s32[3]{0:T(128)} %pad_add_fusion.where_ref, ...), custom_call_target="tpu_custom_call" | custom-call | flops 40249999360 | bytes 1024 | tf_op jit(solution)/shard_map/pallas_call | solution.py:155
  79.1 4.5 %collective-permute-done.10.refs_3_ = bf16[384,192]{1,0:T(8,128)(2,1)S(1)} collective-permute-done((bf16[384,192]{1,0:T(8,128)(2,1)}, bf16[384,192]{1,0:T(8,128)(2,1)S(1)}, u32[]{:S(2)}, u32[]{:S(2)}) %collective-permute-start.10) | collective-permute-done | bytes 147488 | tf_op jit(solution)/shard_map/ppermute | solution.py:30
  86.1 7.0 %shard_map.231 = (f32[384,768]{1,0:T(8,128)}, bf16[384,768]{1,0:T(8,128)(2,1)}, f32[384,128]{1,0:T(8,128)}, bf16[1024,768]{1,0:T(8,128)(2,1)}) custom-call(s32[3]{0:T(128)} %pad_add_fusion.where_ref, bf16[384,192]{1,0:T(8,128)(2,1)} %get-tuple-element.67.refs_0_, bf16[384,192]{1,0:T(8,128)(2,1)} %copy-done.19, bf16[384,192]{1,0:T(8,128)(2,1)} %copy-done.20, ...), custom_call_target="tpu_custom_call" | custom-call | flops 6899999744 | bytes 1024 | tf_op jit(solution)/shard_map/pallas_call | solution.py:45
  93.1 45.7 %all_to_all.20 = bf16[8,128,768]{2,1,0:T(8,128)(2,1)} all-to-all(bf16[8,128,768]{2,1,0:T(8,128)(2,1)} %bitcast.31), channel_id=1, replica_groups=mesh['seq'=4,'fsdp'=8] {'fsdp'}, dimensions={0} | all-to-all | bytes 3145728 | tf_op jit(solution)/shard_map/all_to_all | solution.py:594
  138.8 16.0 %shard_map.232 = (bf16[512,3072]{1,0:T(8,128)(2,1)}, bf16[512,3072]{1,0:T(8,128)(2,1)}, bf16[512,768]{1,0:T(8,128)(2,1)}, bf16[512,768]{1,0:T(8,128)(2,1)}, bf16[1024,768]{1,0:T(8,128)(2,1)}) custom-call(bf16[1024,768]{1,0:T(8,128)(2,1)} %bitcast.30, bf16[768,3072]{1,0:T(8,128)(2,1)} %bitcast.40, bf16[3072,768]{1,0:T(8,128)(2,1)} %bitcast.41), custom_call_target="tpu_custom_call" | custom-call | flops 27599998976 | bytes 1024 | tf_op jit(solution)/shard_map/pallas_call | solution.py:298
  154.8 6.9 %convolution_convert_fusion = bf16[3072,768]{1,0:T(8,128)(2,1)} fusion(bf16[512,3072]{1,0:T(8,128)(2,1)} %get-tuple-element.111, bf16[512,768]{1,0:T(8,128)(2,1)} %get-tuple-element.112), kind=kOutput, calls=%fused_computation | convolution fusion | flops 2418278400 | bytes 8650752 | tf_op jit(solution)/shard_map/dot_general | solution.py:21
  161.7 3.8 %all-to-all-start.1 = ((bf16[8,128,768]{2,1,0:T(8,128)(2,1)}), bf16[8,128,768]{2,1,0:T(8,128)(2,1)S(1)}, u32[]{:S(2)}, u32[]{:S(2)}) async-start(bf16[8,128,768]{2,1,0:T(8,128)(2,1)} %bitcast.12), calls=%async_computation.1 | async-start | bytes 3145728 | tf_op jit(solution)/shard_map/all_to_all | solution.py:594
  165.6 6.7 %convolution_convert_fusion.1 = bf16[768,3072]{1,0:T(8,128)(2,1)} fusion(bf16[512,768]{1,0:T(8,128)(2,1)S(1)} %copy-done.25, bf16[512,3072]{1,0:T(8,128)(2,1)} %get-tuple-element.110), kind=kOutput, calls=%fused_computation.1 | convolution fusion | flops 2418278400 | bytes 8650752 | tf_op jit(solution)/shard_map/dot_general | solution.py:21
  172.4 30.4 %all-to-all-done.1 = bf16[8,128,768]{2,1,0:T(8,128)(2,1)S(1)} async-done(((bf16[8,128,768]{2,1,0:T(8,128)(2,1)}), bf16[8,128,768]{2,1,0:T(8,128)(2,1)S(1)}, u32[]{:S(2)}, u32[]{:S(2)}) %all-to-all-start.1) | async-done | bytes 1572896 | tf_op jit(solution)/shard_map/all_to_all | solution.py:594
  204.0 9.0 %shard_map.233 = (bf16[384,768]{1,0:T(8,128)(2,1)}, f32[384,768]{1,0:T(8,128)}, bf16[768,896]{1,0:T(8,128)(2,1)}, bf16[384,192]{1,0:T(8,128)(2,1)}, bf16[384,192...) custom-call(s32[3]{0:T(128)} %pad_add_fusion.where_ref, ...), custom_call_target="tpu_custom_call" | custom-call | flops 9200000000 | bytes 1024 | tf_op jit(solution)/shard_map/pallas_call | solution.py:45
  214.9 6.1 %collective-permute-done.12.refs_2_ = bf16[384,192]{1,0:T(8,128)(2,1)S(1)} collective-permute-done((bf16[384,192]{1,0:T(8,128)(2,1)}, bf16[384,192]{1,0:T(8,128)(2,1)S(1)}, u32[]{:S(2)}, u32[]{:S(2)}) %collective-permute-start.12) | collective-permute-done | bytes 147488 | tf_op jit(solution)/shard_map/ppermute | solution.py:30
  221.0 3.3 %collective-permute-done.13.refs_3_ = bf16[384,192]{1,0:T(8,128)(2,1)S(1)} collective-permute-done((bf16[384,192]{1,0:T(8,128)(2,1)}, bf16[384,192]{1,0:T(8,128)(2,1)S(1)}, u32[]{:S(2)}, u32[]{:S(2)}) %collective-permute-start.13) | collective-permute-done | bytes 147488 | tf_op jit(solution)/shard_map/ppermute | solution.py:30
  224.3 3.3 %all-to-all-start.2 = ((bf16[32,24,896]{2,1,0:T(8,128)(2,1)}), bf16[32,24,896]{2,1,0:T(8,128)(2,1)S(1)}, u32[]{:S(2)}, u32[]{:S(2)}) async-start(bf16[32,24,896]{2,1,0:T(8,128)(2,1)} %bitcast.32), calls=%async_computation.2 | async-start | bytes 2752512 | tf_op jit(solution)/shard_map/all_to_all | solution.py:703
  227.6 29.0 %shard_map.234 = (bf16[1536,192]{1,0:T(8,128)(2,1)}, f32[192,1536]{1,0:T(8,128)}, f32[192,1536]{1,0:T(8,128)}, f32[3,128,3072]{2,1,0:T(8,128)}) custom-call(s32[3]{0:T(128)} %pad_add_fusion.where_ref, bf16[384,192]{1,0:T(8,128)(2,1)} %get-tuple-element.80.refs_0_, bf16[384,192]{1,0:T(8,128)(2,1)} %copy-done.21, bf16[384,192]{1,0:T(8,128)(2,1)} %copy-done.22, ...), custom_call_target="tpu_custom_call" | custom-call | flops 36800000000 | bytes 1024 | tf_op jit(solution)/shard_map/pallas_call | solution.py:457
  256.6 5.6 %all-to-all-done.2.parts_ref = bf16[32,24,896]{2,1,0:T(8,128)(2,1)S(1)} async-done(((bf16[32,24,896]{2,1,0:T(8,128)(2,1)}), bf16[32,24,896]{2,1,0:T(8,128)(2,1)S(1)}, u32[]{:S(2)}, u32[]{:S(2)}) %all-to-all-start.2) | async-done | bytes 1376288 | tf_op jit(solution)/shard_map/all_to_all | solution.py:703
  262.1 5.8 %shard_map.235 = bf16[768,576]{1,0:T(8,128)(2,1)} custom-call(bf16[1536,768]{1,0:T(8,128)(2,1)} %get-tuple-element.79.normed_ref, bf16[1536,192]{1,0:T(8,128)(2,1)} %get-tuple-element.96.dq_ref, f32[192,1536]{1,0:T(8,128)} %get-tuple-element.94.dkt_ref, f32[192,1536]{1,0:T(8,128)} %get-tuple-element.95.dvt_ref), custom_call_target="tpu_custom_call" | custom-call | flops 6899999744 | bytes 1024 | tf_op jit(solution)/shard_map/pallas_call | solution.py:45
  267.9 3.8 %all-to-all-start.3 = ((bf16[8,96,576]{2,1,0:T(8,128)(2,1)}), bf16[8,96,576]{2,1,0:T(8,128)(2,1)S(1)}, u32[]{:S(2)}, u32[]{:S(2)}) async-start(bf16[8,96,576]{2,1,0:T(8,128)(2,1)} %bitcast.33), calls=%async_computation.3 | async-start | bytes 1966080 | tf_op jit(solution)/shard_map/all_to_all | solution.py:594
  271.7 6.3 %shard_map.236 = (bf16[384,768]{1,0:T(8,128)(2,1)}, bf16[384,768]{1,0:T(8,128)(2,1)}, bf16[384,768]{1,0:T(8,128)(2,1)}, bf16[384,768]{1,0:T(8,128)(2,1)}, f32[1,768]{1,0:T(1,128)}) custom-call(s32[3]{0:T(128)} %pad_add_fusion.where_ref, bf16[1536,768]{1,0:T(8,128)(2,1)} %get-tuple-element.79.normed_ref, bf16[1536,192]{1,0:T(8,128)(2,1)} %get-tuple-element.96.dq_ref, ...), custom_call_target="tpu_custom_call" | custom-call | flops 6899999744 | bytes 1024 | tf_op jit(solution)/shard_map/pallas_call | solution.py:45
  278.1 5.3 %shard_map.238 = f32[8,32]{1,0:T(8,128)} custom-call(f32[3,128,3072]{2,1,0:T(8,128)} %get-tuple-element.107.strip_grad_ref, s32[1,3072]{1,0:T(1,128)} %bitcast.36), custom_call_target="tpu_custom_call" | custom-call | flops 5750000128 | bytes 1024 | tf_op jit(solution)/shard_map/pallas_call | solution.py:45
  304.6 3.5 %shard_map.237 = bf16[384,768]{1,0:T(8,128)(2,1)} custom-call(bf16[384,768]{1,0:T(8,128)(2,1)} %get-tuple-element.100.refs_0_, bf16[384,768]{1,0:T(8,128)(2,1)} %collective-permute-done.14.refs_1_, bf16[384,768]{1,0:T(8,128)(2,1)} %copy-done.14, bf16[384,768]{1,0:T(8,128)(2,1)} %bitcast.48, f32[384,768]{1,0:T(8,128)} %get-tuple-element.104.refs_4_, ...), custom_call_target="tpu_custom_call" | custom-call | flops 3449999872 | bytes 1024 | tf_op jit(solution)/shard_map/pallas_call | solution.py:45
  310.9 2.9 bitcast_convert_fusion.1
  (133 shorter events, 55.2 us)
Async XLA Ops:
  7.2 78.2 %all-gather.2.cloned.1.call-start = ((), (), s32[]{:S(2)}) async-start(), calls=%async_computation.6 | async-start | bytes 1327104 | tf_op jit(solution)/shard_map/all_gather | solution.py:633
  7.2 16.6 %collective-permute-start.1 = (bf16[384,768]{1,0:T(8,128)(2,1)}, bf16[384,768]{1,0:T(8,128)(2,1)S(1)}, u32[]{:S(2)}, u32[]{:S(2)}) collective-permute-start(bf16[384,768]{1,0:T(8,128)(2,1)} %bitcast.44), channel_id=1, source_target_pairs={{0,16},{8,24},{16,0},{24,8},{1,17},{9,25},{17,1},{25,9},{2,18},{10... | collective-permute-start | bytes 1769480 | tf_op jit(solution)/shard_map/ppermute | solution.py:30
  13.9 8.5 %collective-permute-start.3 = (bf16[96,704]{1,0:T(8,128)(2,1)S(1)}, bf16[96,704]{1,0:T(8,128)(2,1)S(1)}, u32[]{:S(2)}, u32[]{:S(2)}) collective-permute-start(bf16[96,704]{1,0:T(8,128)(2,1)S(1)} %concatenate.9.refs_4_), channel_id=1, source_target_pairs={{0,2},{1,3},{2,0},{3,1},{4,6},{5,7},{6,4},{7,5},{8,10},{9,11},{10,... | collective-permute-start | bytes 405512 | tf_op jit(solution)/shard_map/ppermute | solution.py:30
  15.6 13.9 %collective-permute-start.4 = (bf16[96,704]{1,0:T(8,128)(2,1)S(1)}, bf16[96,704]{1,0:T(8,128)(2,1)S(1)}, u32[]{:S(2)}, u32[]{:S(2)}) collective-permute-start(bf16[96,704]{1,0:T(8,128)(2,1)S(1)} %concatenate.9.refs_4_), channel_id=1, source_target_pairs={{0,4},{1,5},{2,6},{3,7},{4,0},{5,1},{6,2},{7,3},{8,12},{9,13},{10,... | collective-permute-start | bytes 405512 | tf_op jit(solution)/shard_map/ppermute | solution.py:30
  18.2 11.3 %collective-permute-start.5 = (bf16[96,704]{1,0:T(8,128)(2,1)S(1)}, bf16[96,704]{1,0:T(8,128)(2,1)S(1)}, u32[]{:S(2)}, u32[]{:S(2)}) collective-permute-start(bf16[96,704]{1,0:T(8,128)(2,1)S(1)} %concatenate.9.refs_4_), channel_id=1, source_target_pairs={{0,6},{1,7},{2,4},{3,5},{4,2},{5,3},{6,0},{7,1},{8,14},{9,15},{10,... | collective-permute-start | bytes 405512 | tf_op jit(solution)/shard_map/ppermute | solution.py:30
  18.4 17.6 %collective-permute-start.6 = (bf16[96,704]{1,0:T(8,128)(2,1)S(1)}, bf16[96,704]{1,0:T(8,128)(2,1)S(1)}, u32[]{:S(2)}, u32[]{:S(2)}) collective-permute-start(bf16[96,704]{1,0:T(8,128)(2,1)S(1)} %concatenate.9.refs_4_), channel_id=1, source_target_pairs={{0,1},{1,0},{2,3},{3,2},{4,5},{5,4},{6,7},{7,6},{8,9},{9,8},{10,11... | collective-permute-start | bytes 405512 | tf_op jit(solution)/shard_map/ppermute | solution.py:30
  22.5 16.1 %collective-permute-start = (bf16[384,768]{1,0:T(8,128)(2,1)}, bf16[384,768]{1,0:T(8,128)(2,1)S(1)}, u32[]{:S(2)}, u32[]{:S(2)}) collective-permute-start(bf16[384,768]{1,0:T(8,128)(2,1)} %bitcast.45), channel_id=1, source_target_pairs={{0,8},{8,0},{16,24},{24,16},{1,9},{9,1},{17,25},{25,17},{2,10},{10... | collective-permute-start | bytes 1769480 | tf_op jit(solution)/shard_map/ppermute | solution.py:30
  23.8 14.7 %collective-permute-start.2 = (bf16[384,768]{1,0:T(8,128)(2,1)S(1)}, bf16[384,768]{1,0:T(8,128)(2,1)S(1)}, u32[]{:S(2)}, u32[]{:S(2)}) collective-permute-start(bf16[384,768]{1,0:T(8,128)(2,1)S(1)} %collective-permute-done.1.refs_2_), channel_id=1, source_target_pairs={{0,8},{8,0},{16,24},{24,16},{1,9},{9,1},{17,25},{25,17},{2,10},{10... | collective-permute-start | bytes 1769480 | tf_op jit(solution)/shard_map/ppermute | solution.py:30
  29.5 9.0 %collective-permute-start.7 = (bf16[288,704]{1,0:T(8,128)(2,1)S(1)}, bf16[288,704]{1,0:T(8,128)(2,1)S(1)}, u32[]{:S(2)}, u32[]{:S(2)}) collective-permute-start(bf16[288,704]{1,0:T(8,128)(2,1)S(1)} %pad_maximum_fusion), channel_id=1, source_target_pairs={{0,1},{1,0},{2,3},{3,2},{4,5},{5,4},{6,7},{7,6},{8,9},{9,8},{10,11... | collective-permute-start | bytes 1216520 | tf_op jit(solution)/shard_map/ppermute | solution.py:30
  38.6 269.5 %reduce-scatter.5.cloned.1.call-start = ((), (), s32[]{:S(2)}) async-start(), calls=%async_computation.8 | async-start | bytes 5898240 | tf_op jit(solution)/shard_map/reduce_scatter | solution.py:667
  76.0 7.5 %collective-permute-start.10 = (bf16[384,192]{1,0:T(8,128)(2,1)}, bf16[384,192]{1,0:T(8,128)(2,1)S(1)}, u32[]{:S(2)}, u32[]{:S(2)}) collective-permute-start(bf16[384,192]{1,0:T(8,128)(2,1)} %get-tuple-element.70), channel_id=1, source_target_pairs={{0,24},{8,16},{16,8},{24,0},{1,25},{9,17},{17,9},{25,1},{2,26},{10... | collective-permute-start | bytes 442376 | tf_op jit(solution)/shard_map/ppermute | solution.py:30
  76.1 7.5 %collective-permute-start.8 = (bf16[384,192]{1,0:T(8,128)(2,1)}, bf16[384,192]{1,0:T(8,128)(2,1)S(1)}, u32[]{:S(2)}, u32[]{:S(2)}) collective-permute-start(bf16[384,192]{1,0:T(8,128)(2,1)} %get-tuple-element.68), channel_id=1, source_target_pairs={{0,8},{8,0},{16,24},{24,16},{1,9},{9,1},{17,25},{25,17},{2,10},{10... | collective-permute-start | bytes 442376 | tf_op jit(solution)/shard_map/ppermute | solution.py:30
  76.3 9.1 %collective-permute-start.9 = (bf16[384,192]{1,0:T(8,128)(2,1)}, bf16[384,192]{1,0:T(8,128)(2,1)S(1)}, u32[]{:S(2)}, u32[]{:S(2)}) collective-permute-start(bf16[384,192]{1,0:T(8,128)(2,1)} %get-tuple-element.69), channel_id=1, source_target_pairs={{0,16},{8,24},{16,0},{24,8},{1,17},{9,25},{17,1},{25,9},{2,18},{10... | collective-permute-start | bytes 442376 | tf_op jit(solution)/shard_map/ppermute | solution.py:30
  161.7 41.1 %all-to-all-start.1 = ((bf16[8,128,768]{2,1,0:T(8,128)(2,1)}), bf16[8,128,768]{2,1,0:T(8,128)(2,1)S(1)}, u32[]{:S(2)}, u32[]{:S(2)}) async-start(bf16[8,128,768]{2,1,0:T(8,128)(2,1)} %bitcast.12), calls=%async_computation.1 | async-start | bytes 3145728 | tf_op jit(solution)/shard_map/all_to_all | solution.py:594
  165.6 145.4 %reduce-scatter.3.cloned.1.call-start = ((), (), s32[]{:S(2)}) async-start(), calls=%async_computation.7 | async-start | bytes 5898240 | tf_op jit(solution)/shard_map/reduce_scatter | solution.py:666
  213.0 8.0 %collective-permute-start.12 = (bf16[384,192]{1,0:T(8,128)(2,1)}, bf16[384,192]{1,0:T(8,128)(2,1)S(1)}, u32[]{:S(2)}, u32[]{:S(2)}) collective-permute-start(bf16[384,192]{1,0:T(8,128)(2,1)} %get-tuple-element.82), channel_id=1, source_target_pairs={{0,16},{8,24},{16,0},{24,8},{1,17},{9,25},{17,1},{25,9},{2,18},{10... | collective-permute-start | bytes 442376 | tf_op jit(solution)/shard_map/ppermute | solution.py:30
  214.0 10.3 %collective-permute-start.13 = (bf16[384,192]{1,0:T(8,128)(2,1)}, bf16[384,192]{1,0:T(8,128)(2,1)S(1)}, u32[]{:S(2)}, u32[]{:S(2)}) collective-permute-start(bf16[384,192]{1,0:T(8,128)(2,1)} %get-tuple-element.83), channel_id=1, source_target_pairs={{0,24},{8,16},{16,8},{24,0},{1,25},{9,17},{17,9},{25,1},{2,26},{10... | collective-permute-start | bytes 442376 | tf_op jit(solution)/shard_map/ppermute | solution.py:30
  224.3 37.9 %all-to-all-start.2 = ((bf16[32,24,896]{2,1,0:T(8,128)(2,1)}), bf16[32,24,896]{2,1,0:T(8,128)(2,1)S(1)}, u32[]{:S(2)}, u32[]{:S(2)}) async-start(bf16[32,24,896]{2,1,0:T(8,128)(2,1)} %bitcast.32), calls=%async_computation.2 | async-start | bytes 2752512 | tf_op jit(solution)/shard_map/all_to_all | solution.py:703
  267.9 45.9 %all-to-all-start.3 = ((bf16[8,96,576]{2,1,0:T(8,128)(2,1)}), bf16[8,96,576]{2,1,0:T(8,128)(2,1)S(1)}, u32[]{:S(2)}, u32[]{:S(2)}) async-start(bf16[8,96,576]{2,1,0:T(8,128)(2,1)} %bitcast.33), calls=%async_computation.3 | async-start | bytes 1966080 | tf_op jit(solution)/shard_map/all_to_all | solution.py:594
  278.1 8.4 %collective-permute-start.15 = (bf16[384,768]{1,0:T(8,128)(2,1)}, bf16[384,768]{1,0:T(8,128)(2,1)S(1)}, u32[]{:S(2)}, u32[]{:S(2)}) collective-permute-start(bf16[384,768]{1,0:T(8,128)(2,1)} %get-tuple-element.103), channel_id=1, source_target_pairs={{0,8},{8,0},{16,24},{24,16},{1,9},{9,1},{17,25},{25,17},{2,10},{10... | collective-permute-start | bytes 1769480 | tf_op jit(solution)/shard_map/ppermute | solution.py:30
  286.3 17.5 %collective-permute-start.14 = (bf16[384,768]{1,0:T(8,128)(2,1)S(1)}, bf16[384,768]{1,0:T(8,128)(2,1)}, u32[]{:S(2)}, u32[]{:S(2)}) collective-permute-start(bf16[384,768]{1,0:T(8,128)(2,1)S(1)} %copy-done.13), channel_id=1, source_target_pairs={{0,8},{8,0},{16,24},{24,16},{1,9},{9,1},{17,25},{25,17},{2,10},{10... | collective-permute-start | bytes 1769480 | tf_op jit(solution)/shard_map/ppermute | solution.py:30
  286.6 17.2 %collective-permute-start.16 = (bf16[384,768]{1,0:T(8,128)(2,1)S(1)}, bf16[384,768]{1,0:T(8,128)(2,1)S(1)}, u32[]{:S(2)}, u32[]{:S(2)}) collective-permute-start(bf16[384,768]{1,0:T(8,128)(2,1)S(1)} %add_convert_fusion), channel_id=1, source_target_pairs={{0,16},{8,24},{16,0},{24,8},{1,17},{9,25},{17,1},{25,9},{2,18},{10... | collective-permute-start | bytes 1769480 | tf_op jit(solution)/shard_map/ppermute | solution.py:30
  291.6 4.6 %collective-permute-start.19 = (f32[864]{0:T(1024)S(1)}, f32[864]{0:T(1024)S(1)}, u32[]{:S(2)}, u32[]{:S(2)}) collective-permute-start(f32[864]{0:T(1024)S(1)} %add.40), channel_id=1, source_target_pairs={{0,4},{1,5},{2,6},{3,7},{4,0},{5,1},{6,2},{7,3},{8,12},{9,13},{10,... | collective-permute-start | bytes 10376 | tf_op jit(solution)/shard_map/ppermute | solution.py:30
  298.4 4.8 %collective-permute-start.21 = (f32[768]{0:T(1024)S(1)}, f32[768]{0:T(1024)S(1)}, u32[]{:S(2)}, u32[]{:S(2)}) collective-permute-start(f32[768]{0:T(1024)S(1)} %slice_add_fusion), channel_id=1, source_target_pairs={{0,16},{8,24},{16,0},{24,8},{1,17},{9,25},{17,1},{25,9},{2,18},{10... | collective-permute-start | bytes 9224 | tf_op jit(solution)/shard_map/ppermute | solution.py:30
  (30 other events, 188.5 us)
Sparse Core Ops, SparseCore 0:
  38.7 42.7 all-gather.1
  161.8 46.9 reduce-scatter.4
  211.5 60.5 reduce-scatter.2
where the time goes:
time: 327 us; the launch traced here: 324 us
  Pallas kernels  127 us (39%)
  waiting for transfers between devices  65.6 us (20%)
  blocking collectives  45.7 us (14%)
  starting transfers between devices  35 us (11%)
  local copies, waits for them, and re-layouts  16.2 us (5%)
  between operations  14.3 us (4%)
  matrix products  13.6 us (4%)
  other arithmetic  6.54 us (2%)
    all_to_all x1, blocking collectives, exchange(): return lax.all_to_all(split, 'fsdp', 0, 0, tiled=True)  45.7 us
    pallas_call x9, Pallas kernels, call(): pl.pallas_call(kernel, in_specs=specs, out_specs=[pl.BlockSpec(memory_spa...  45.4 us
    pallas_call x1, Pallas kernels, forward_attention(): pl.pallas_call(functools.partial(forward_kernel, heads=heads, size=size,...  36.3 us
    all_to_all x2, waiting for transfers between devices, exchange(): return lax.all_to_all(split, 'fsdp', 0, 0, tiled=True)  30.4 us
    ppermute x22, waiting for transfers between devices, swap(): return lax.ppermute(values, axis, [(i, i ^ offset) for i in range(count)])  29.6 us
    pallas_call x1, Pallas kernels, backward_attention(): pl.pallas_call(functools.partial(attend_back_kernel, heads=heads, size=wi...  29 us
    ppermute x22, starting transfers between devices, swap(): return lax.ppermute(values, axis, [(i, i ^ offset) for i in range(count)])  23.4 us
    pallas_call x1, Pallas kernels, expert_step(): pl.pallas_call(functools.partial(expert_kernel, sources=sources), grid=(u...  16 us
  transfers between devices with their start and end apart: 28, of which 12 were waited for; matrix products, arithmetic and copies ran while one was open for 8% of the time, Pallas kernels for 31%

commit v1 on v0

--- a/solution.py
+++ b/solution.py
@@ -706,11 +706,12 @@
     dq, dkt, dvt, strip_grad = backward_attention(
         where, mixed_grads, q, k, v, o32, shares, attention, strip.shape
     )
-    dq, output_terms = lax.optimization_barrier((dq, output_terms))
     (weight_terms,) = call(
         weight_kernel, [normed, dq, dkt, dvt], [((features, 3 * width), LOW)], time=6
     )
-    held_dq, weight_terms = lax.optimization_barrier((dq, weight_terms))
+    held_dq, weight_terms, output_terms = lax.optimization_barrier(
+        (dq, weight_terms, output_terms)
+    )
     weight_terms = exchange(weight_terms)
     results = call(
         functools.partial(row_kernel, seq_count=seq_count),

time: 327 us -> 324 us (level)
  waiting for transfers between devices: 65.6 us -> 60 us
    all_to_all x1, waiting for transfers between devices: 5.57 us -> 0.29 us  [on_device(): lax.all_to_all(held.reshape(device_count, share, features + 128), both, 0...]
  transfers between devices with their start and end apart: 28 -> 28, of which waited for: 12 -> 11; matrix products, arithmetic and copies ran while one was open for 8% -> 8% of each run, Pallas kernels for 31% -> 32%
where the time goes in v1:
time: 324 us; the launch traced here: 321 us
  Pallas kernels  126 us (39%)
  waiting for transfers between devices  60 us (19%)
  blocking collectives  45.7 us (14%)
  starting transfers between devices  38 us (12%)
  local copies, waits for them, and re-layouts  16.2 us (5%)
  between operations  14.3 us (4%)
  matrix products  13.6 us (4%)
  other arithmetic  6.54 us (2%)
    all_to_all x1, blocking collectives, exchange(): return lax.all_to_all(split, 'fsdp', 0, 0, tiled=True)  45.7 us
    pallas_call x9, Pallas kernels, call(): pl.pallas_call(kernel, in_specs=specs, out_specs=[pl.BlockSpec(memory_spa...  44.9 us
    pallas_call x1, Pallas kernels, forward_attention(): pl.pallas_call(functools.partial(forward_kernel, heads=heads, size=size,...  36.3 us
    all_to_all x2, waiting for transfers between devices, exchange(): return lax.all_to_all(split, 'fsdp', 0, 0, tiled=True)  30.4 us
    ppermute x22, waiting for transfers between devices, swap(): return lax.ppermute(values, axis, [(i, i ^ offset) for i in range(count)])  29.2 us
    pallas_call x1, Pallas kernels, backward_attention(): pl.pallas_call(functools.partial(attend_back_kernel, heads=heads, size=wi...  29 us
    ppermute x22, starting transfers between devices, swap(): return lax.ppermute(values, axis, [(i, i ^ offset) for i in range(count)])  24.3 us
    pallas_call x1, Pallas kernels, expert_step(): pl.pallas_call(functools.partial(expert_kernel, sources=sources), grid=(u...  16 us
  transfers between devices with their start and end apart: 28, of which 11 were waited for; matrix products, arithmetic and copies ran while one was open for 8% of the time, Pallas kernels for 32%

profile of v1, /device:TPU:0, one launch (start us, length us, event | category | flops | bytes accessed | tf_op | source)
XLA Modules:
  0.0 320.5 jit_solution(4795529343656324945)
XLA Ops:
  7.2 3.0 collective-permute-start.1
  23.8 5.6 %collective-permute-done.4.refs_6_ = bf16[96,704]{1,0:T(8,128)(2,1)S(1)} collective-permute-done((bf16[96,704]{1,0:T(8,128)(2,1)S(1)}, bf16[96,704]{1,0:T(8,128)(2,1)S(1)}, u32[]{:S(2)}, u32[]{:S(2)}) %collective-permute-start.4) | collective-permute-done | bytes 135200 | tf_op jit(solution)/shard_map/ppermute | solution.py:30
  31.0 4.3 %shard_map.229.refs_10_ = f32[3,128,3072]{2,1,0:T(8,128)} custom-call(bf16[16,32]{1,0:T(8,128)(2,1)} %pad.8.table_ref, s32[1,3072]{1,0:T(1,128)} %bitcast.35), custom_call_target="tpu_custom_call" | custom-call | flops 4600000000 | bytes 1024 | tf_op jit(solution)/shard_map/pallas_call | solution.py:45
  39.7 36.3 %shard_map.230 = (bf16[1536,768]{1,0:T(8,128)(2,1)}, bf16[1536,192]{1,0:T(8,128)(2,1)}, bf16[1536,192]{1,0:T(8,128)(2,1)}, bf16[1536,192]{1,0:T(8,128)(2,1)}, bf...) custom-call(s32[3]{0:T(128)} %pad_add_fusion.where_ref, ...), custom_call_target="tpu_custom_call" | custom-call | flops 40249999360 | bytes 1024 | tf_op jit(solution)/shard_map/pallas_call | solution.py:155
  79.1 4.5 %collective-permute-done.10.refs_3_ = bf16[384,192]{1,0:T(8,128)(2,1)S(1)} collective-permute-done((bf16[384,192]{1,0:T(8,128)(2,1)}, bf16[384,192]{1,0:T(8,128)(2,1)S(1)}, u32[]{:S(2)}, u32[]{:S(2)}) %collective-permute-start.10) | collective-permute-done | bytes 147488 | tf_op jit(solution)/shard_map/ppermute | solution.py:30
  86.1 7.0 %shard_map.231 = (f32[384,768]{1,0:T(8,128)}, bf16[384,768]{1,0:T(8,128)(2,1)}, f32[384,128]{1,0:T(8,128)}, bf16[1024,768]{1,0:T(8,128)(2,1)}) custom-call(s32[3]{0:T(128)} %pad_add_fusion.where_ref, bf16[384,192]{1,0:T(8,128)(2,1)} %get-tuple-element.66.refs_0_, bf16[384,192]{1,0:T(8,128)(2,1)} %copy-done.19, bf16[384,192]{1,0:T(8,128)(2,1)} %copy-done.20, ...), custom_call_target="tpu_custom_call" | custom-call | flops 6899999744 | bytes 1024 | tf_op jit(solution)/shard_map/pallas_call | solution.py:45
  93.1 45.7 %all_to_all.20 = bf16[8,128,768]{2,1,0:T(8,128)(2,1)} all-to-all(bf16[8,128,768]{2,1,0:T(8,128)(2,1)} %bitcast.31), channel_id=1, replica_groups=mesh['seq'=4,'fsdp'=8] {'fsdp'}, dimensions={0} | all-to-all | bytes 3145728 | tf_op jit(solution)/shard_map/all_to_all | solution.py:594
  138.8 16.0 %shard_map.232 = (bf16[512,3072]{1,0:T(8,128)(2,1)}, bf16[512,3072]{1,0:T(8,128)(2,1)}, bf16[512,768]{1,0:T(8,128)(2,1)}, bf16[512,768]{1,0:T(8,128)(2,1)}, bf16[1024,768]{1,0:T(8,128)(2,1)}) custom-call(bf16[1024,768]{1,0:T(8,128)(2,1)} %bitcast.30, bf16[768,3072]{1,0:T(8,128)(2,1)} %bitcast.40, bf16[3072,768]{1,0:T(8,128)(2,1)} %bitcast.41), custom_call_target="tpu_custom_call" | custom-call | flops 27599998976 | bytes 1024 | tf_op jit(solution)/shard_map/pallas_call | solution.py:298
  154.8 6.9 %convolution_convert_fusion = bf16[3072,768]{1,0:T(8,128)(2,1)} fusion(bf16[512,3072]{1,0:T(8,128)(2,1)} %get-tuple-element.109, bf16[512,768]{1,0:T(8,128)(2,1)} %get-tuple-element.110), kind=kOutput, calls=%fused_computation | convolution fusion | flops 2418278400 | bytes 8650752 | tf_op jit(solution)/shard_map/dot_general | solution.py:21
  161.7 3.8 %all-to-all-start.1 = ((bf16[8,128,768]{2,1,0:T(8,128)(2,1)}), bf16[8,128,768]{2,1,0:T(8,128)(2,1)S(1)}, u32[]{:S(2)}, u32[]{:S(2)}) async-start(bf16[8,128,768]{2,1,0:T(8,128)(2,1)} %bitcast.12), calls=%async_computation.1 | async-start | bytes 3145728 | tf_op jit(solution)/shard_map/all_to_all | solution.py:594
  165.6 6.7 %convolution_convert_fusion.1 = bf16[768,3072]{1,0:T(8,128)(2,1)} fusion(bf16[512,768]{1,0:T(8,128)(2,1)S(1)} %copy-done.25, bf16[512,3072]{1,0:T(8,128)(2,1)} %get-tuple-element.108), kind=kOutput, calls=%fused_computation.1 | convolution fusion | flops 2418278400 | bytes 8650752 | tf_op jit(solution)/shard_map/dot_general | solution.py:21
  172.4 30.4 %all-to-all-done.1 = bf16[8,128,768]{2,1,0:T(8,128)(2,1)S(1)} async-done(((bf16[8,128,768]{2,1,0:T(8,128)(2,1)}), bf16[8,128,768]{2,1,0:T(8,128)(2,1)S(1)}, u32[]{:S(2)}, u32[]{:S(2)}) %all-to-all-start.1) | async-done | bytes 1572896 | tf_op jit(solution)/shard_map/all_to_all | solution.py:594
  204.0 9.0 %shard_map.233 = (bf16[384,768]{1,0:T(8,128)(2,1)}, f32[384,768]{1,0:T(8,128)}, bf16[768,896]{1,0:T(8,128)(2,1)}, bf16[384,192]{1,0:T(8,128)(2,1)}, bf16[384,192...) custom-call(s32[3]{0:T(128)} %pad_add_fusion.where_ref, ...), custom_call_target="tpu_custom_call" | custom-call | flops 9200000000 | bytes 1024 | tf_op jit(solution)/shard_map/pallas_call | solution.py:45
  214.9 6.1 %collective-permute-done.12.refs_2_ = bf16[384,192]{1,0:T(8,128)(2,1)S(1)} collective-permute-done((bf16[384,192]{1,0:T(8,128)(2,1)}, bf16[384,192]{1,0:T(8,128)(2,1)S(1)}, u32[]{:S(2)}, u32[]{:S(2)}) %collective-permute-start.12) | collective-permute-done | bytes 147488 | tf_op jit(solution)/shard_map/ppermute | solution.py:30
  221.0 3.3 %collective-permute-done.13.refs_3_ = bf16[384,192]{1,0:T(8,128)(2,1)S(1)} collective-permute-done((bf16[384,192]{1,0:T(8,128)(2,1)}, bf16[384,192]{1,0:T(8,128)(2,1)S(1)}, u32[]{:S(2)}, u32[]{:S(2)}) %collective-permute-start.13) | collective-permute-done | bytes 147488 | tf_op jit(solution)/shard_map/ppermute | solution.py:30
  224.3 3.3 %all-to-all-start.2 = ((bf16[32,24,896]{2,1,0:T(8,128)(2,1)}), bf16[32,24,896]{2,1,0:T(8,128)(2,1)S(1)}, u32[]{:S(2)}, u32[]{:S(2)}) async-start(bf16[32,24,896]{2,1,0:T(8,128)(2,1)} %bitcast.32), calls=%async_computation.2 | async-start | bytes 2752512 | tf_op jit(solution)/shard_map/all_to_all | solution.py:703
  227.6 29.0 %shard_map.234 = (bf16[1536,192]{1,0:T(8,128)(2,1)}, f32[192,1536]{1,0:T(8,128)}, f32[192,1536]{1,0:T(8,128)}, f32[3,128,3072]{2,1,0:T(8,128)}) custom-call(s32[3]{0:T(128)} %pad_add_fusion.where_ref, bf16[384,192]{1,0:T(8,128)(2,1)} %get-tuple-element.79.refs_0_, bf16[384,192]{1,0:T(8,128)(2,1)} %copy-done.21, bf16[384,192]{1,0:T(8,128)(2,1)} %copy-done.22, ...), custom_call_target="tpu_custom_call" | custom-call | flops 36800000000 | bytes 1024 | tf_op jit(solution)/shard_map/pallas_call | solution.py:457
  256.6 5.3 %shard_map.235 = bf16[768,576]{1,0:T(8,128)(2,1)} custom-call(bf16[1536,768]{1,0:T(8,128)(2,1)} %get-tuple-element.78.normed_ref, bf16[1536,192]{1,0:T(8,128)(2,1)} %get-tuple-element.94.dq_ref, f32[192,1536]{1,0:T(8,128)} %get-tuple-element.90.dkt_ref, f32[192,1536]{1,0:T(8,128)} %get-tuple-element.91.dvt_ref), custom_call_target="tpu_custom_call" | custom-call | flops 6899999744 | bytes 1024 | tf_op jit(solution)/shard_map/pallas_call | solution.py:45
  262.1 6.0 %all-to-all-start.3 = ((bf16[8,96,576]{2,1,0:T(8,128)(2,1)}), bf16[8,96,576]{2,1,0:T(8,128)(2,1)S(1)}, u32[]{:S(2)}, u32[]{:S(2)}) async-start(bf16[8,96,576]{2,1,0:T(8,128)(2,1)} %bitcast.33), calls=%async_computation.3 | async-start | bytes 1966080 | tf_op jit(solution)/shard_map/all_to_all | solution.py:594
  268.2 6.3 %shard_map.236 = (bf16[384,768]{1,0:T(8,128)(2,1)}, bf16[384,768]{1,0:T(8,128)(2,1)}, bf16[384,768]{1,0:T(8,128)(2,1)}, bf16[384,768]{1,0:T(8,128)(2,1)}, f32[1,768]{1,0:T(1,128)}) custom-call(s32[3]{0:T(128)} %pad_add_fusion.where_ref, bf16[1536,768]{1,0:T(8,128)(2,1)} %get-tuple-element.78.normed_ref, bf16[1536,192]{1,0:T(8,128)(2,1)} %get-tuple-element.94.dq_ref, ...), custom_call_target="tpu_custom_call" | custom-call | flops 6899999744 | bytes 1024 | tf_op jit(solution)/shard_map/pallas_call | solution.py:45
  274.5 5.3 %shard_map.238 = f32[8,32]{1,0:T(8,128)} custom-call(f32[3,128,3072]{2,1,0:T(8,128)} %get-tuple-element.105.strip_grad_ref, s32[1,3072]{1,0:T(1,128)} %bitcast.36), custom_call_target="tpu_custom_call" | custom-call | flops 5750000128 | bytes 1024 | tf_op jit(solution)/shard_map/pallas_call | solution.py:45
  301.5 3.5 %shard_map.237 = bf16[384,768]{1,0:T(8,128)(2,1)} custom-call(bf16[384,768]{1,0:T(8,128)(2,1)} %get-tuple-element.98.refs_0_, bf16[384,768]{1,0:T(8,128)(2,1)} %collective-permute-done.14.refs_1_, bf16[384,768]{1,0:T(8,128)(2,1)} %copy-done.14, bf16[384,768]{1,0:T(8,128)(2,1)} %bitcast.48, f32[384,768]{1,0:T(8,128)} %get-tuple-element.102.refs_4_, ...), custom_call_target="tpu_custom_call" | custom-call | flops 3449999872 | bytes 1024 | tf_op jit(solution)/shard_map/pallas_call | solution.py:45
  305.0 2.8 bitcast_convert_fusion
  307.8 2.9 bitcast_convert_fusion.1
  (133 shorter events, 53.1 us)
Async XLA Ops:
  7.2 78.2 %all-gather.2.cloned.1.call-start = ((), (), s32[]{:S(2)}) async-start(), calls=%async_computation.6 | async-start | bytes 1327104 | tf_op jit(solution)/shard_map/all_gather | solution.py:633
  7.2 16.6 %collective-permute-start.1 = (bf16[384,768]{1,0:T(8,128)(2,1)}, bf16[384,768]{1,0:T(8,128)(2,1)S(1)}, u32[]{:S(2)}, u32[]{:S(2)}) collective-permute-start(bf16[384,768]{1,0:T(8,128)(2,1)} %bitcast.44), channel_id=1, source_target_pairs={{0,16},{8,24},{16,0},{24,8},{1,17},{9,25},{17,1},{25,9},{2,18},{10... | collective-permute-start | bytes 1769480 | tf_op jit(solution)/shard_map/ppermute | solution.py:30
  13.9 8.5 %collective-permute-start.3 = (bf16[96,704]{1,0:T(8,128)(2,1)S(1)}, bf16[96,704]{1,0:T(8,128)(2,1)S(1)}, u32[]{:S(2)}, u32[]{:S(2)}) collective-permute-start(bf16[96,704]{1,0:T(8,128)(2,1)S(1)} %concatenate.9.refs_4_), channel_id=1, source_target_pairs={{0,2},{1,3},{2,0},{3,1},{4,6},{5,7},{6,4},{7,5},{8,10},{9,11},{10,... | collective-permute-start | bytes 405512 | tf_op jit(solution)/shard_map/ppermute | solution.py:30
  15.6 13.9 %collective-permute-start.4 = (bf16[96,704]{1,0:T(8,128)(2,1)S(1)}, bf16[96,704]{1,0:T(8,128)(2,1)S(1)}, u32[]{:S(2)}, u32[]{:S(2)}) collective-permute-start(bf16[96,704]{1,0:T(8,128)(2,1)S(1)} %concatenate.9.refs_4_), channel_id=1, source_target_pairs={{0,4},{1,5},{2,6},{3,7},{4,0},{5,1},{6,2},{7,3},{8,12},{9,13},{10,... | collective-permute-start | bytes 405512 | tf_op jit(solution)/shard_map/ppermute | solution.py:30
  18.2 11.3 %collective-permute-start.5 = (bf16[96,704]{1,0:T(8,128)(2,1)S(1)}, bf16[96,704]{1,0:T(8,128)(2,1)S(1)}, u32[]{:S(2)}, u32[]{:S(2)}) collective-permute-start(bf16[96,704]{1,0:T(8,128)(2,1)S(1)} %concatenate.9.refs_4_), channel_id=1, source_target_pairs={{0,6},{1,7},{2,4},{3,5},{4,2},{5,3},{6,0},{7,1},{8,14},{9,15},{10,... | collective-permute-start | bytes 405512 | tf_op jit(solution)/shard_map/ppermute | solution.py:30
  18.4 17.6 %collective-permute-start.6 = (bf16[96,704]{1,0:T(8,128)(2,1)S(1)}, bf16[96,704]{1,0:T(8,128)(2,1)S(1)}, u32[]{:S(2)}, u32[]{:S(2)}) collective-permute-start(bf16[96,704]{1,0:T(8,128)(2,1)S(1)} %concatenate.9.refs_4_), channel_id=1, source_target_pairs={{0,1},{1,0},{2,3},{3,2},{4,5},{5,4},{6,7},{7,6},{8,9},{9,8},{10,11... | collective-permute-start | bytes 405512 | tf_op jit(solution)/shard_map/ppermute | solution.py:30
  22.5 16.1 %collective-permute-start = (bf16[384,768]{1,0:T(8,128)(2,1)}, bf16[384,768]{1,0:T(8,128)(2,1)S(1)}, u32[]{:S(2)}, u32[]{:S(2)}) collective-permute-start(bf16[384,768]{1,0:T(8,128)(2,1)} %bitcast.45), channel_id=1, source_target_pairs={{0,8},{8,0},{16,24},{24,16},{1,9},{9,1},{17,25},{25,17},{2,10},{10... | collective-permute-start | bytes 1769480 | tf_op jit(solution)/shard_map/ppermute | solution.py:30
  23.8 14.7 %collective-permute-start.2 = (bf16[384,768]{1,0:T(8,128)(2,1)S(1)}, bf16[384,768]{1,0:T(8,128)(2,1)S(1)}, u32[]{:S(2)}, u32[]{:S(2)}) collective-permute-start(bf16[384,768]{1,0:T(8,128)(2,1)S(1)} %collective-permute-done.1.refs_2_), channel_id=1, source_target_pairs={{0,8},{8,0},{16,24},{24,16},{1,9},{9,1},{17,25},{25,17},{2,10},{10... | collective-permute-start | bytes 1769480 | tf_op jit(solution)/shard_map/ppermute | solution.py:30
  29.5 9.0 %collective-permute-start.7 = (bf16[288,704]{1,0:T(8,128)(2,1)S(1)}, bf16[288,704]{1,0:T(8,128)(2,1)S(1)}, u32[]{:S(2)}, u32[]{:S(2)}) collective-permute-start(bf16[288,704]{1,0:T(8,128)(2,1)S(1)} %pad_maximum_fusion), channel_id=1, source_target_pairs={{0,1},{1,0},{2,3},{3,2},{4,5},{5,4},{6,7},{7,6},{8,9},{9,8},{10,11... | collective-permute-start | bytes 1216520 | tf_op jit(solution)/shard_map/ppermute | solution.py:30
  38.6 266.4 %reduce-scatter.5.cloned.1.call-start = ((), (), s32[]{:S(2)}) async-start(), calls=%async_computation.8 | async-start | bytes 5898240 | tf_op jit(solution)/shard_map/reduce_scatter | solution.py:667
  76.0 7.5 %collective-permute-start.10 = (bf16[384,192]{1,0:T(8,128)(2,1)}, bf16[384,192]{1,0:T(8,128)(2,1)S(1)}, u32[]{:S(2)}, u32[]{:S(2)}) collective-permute-start(bf16[384,192]{1,0:T(8,128)(2,1)} %get-tuple-element.69), channel_id=1, source_target_pairs={{0,24},{8,16},{16,8},{24,0},{1,25},{9,17},{17,9},{25,1},{2,26},{10... | collective-permute-start | bytes 442376 | tf_op jit(solution)/shard_map/ppermute | solution.py:30
  76.1 7.5 %collective-permute-start.8 = (bf16[384,192]{1,0:T(8,128)(2,1)}, bf16[384,192]{1,0:T(8,128)(2,1)S(1)}, u32[]{:S(2)}, u32[]{:S(2)}) collective-permute-start(bf16[384,192]{1,0:T(8,128)(2,1)} %get-tuple-element.67), channel_id=1, source_target_pairs={{0,8},{8,0},{16,24},{24,16},{1,9},{9,1},{17,25},{25,17},{2,10},{10... | collective-permute-start | bytes 442376 | tf_op jit(solution)/shard_map/ppermute | solution.py:30
  76.3 9.1 %collective-permute-start.9 = (bf16[384,192]{1,0:T(8,128)(2,1)}, bf16[384,192]{1,0:T(8,128)(2,1)S(1)}, u32[]{:S(2)}, u32[]{:S(2)}) collective-permute-start(bf16[384,192]{1,0:T(8,128)(2,1)} %get-tuple-element.68), channel_id=1, source_target_pairs={{0,16},{8,24},{16,0},{24,8},{1,17},{9,25},{17,1},{25,9},{2,18},{10... | collective-permute-start | bytes 442376 | tf_op jit(solution)/shard_map/ppermute | solution.py:30
  161.7 41.1 %all-to-all-start.1 = ((bf16[8,128,768]{2,1,0:T(8,128)(2,1)}), bf16[8,128,768]{2,1,0:T(8,128)(2,1)S(1)}, u32[]{:S(2)}, u32[]{:S(2)}) async-start(bf16[8,128,768]{2,1,0:T(8,128)(2,1)} %bitcast.12), calls=%async_computation.1 | async-start | bytes 3145728 | tf_op jit(solution)/shard_map/all_to_all | solution.py:594
  165.6 142.3 %reduce-scatter.3.cloned.1.call-start = ((), (), s32[]{:S(2)}) async-start(), calls=%async_computation.7 | async-start | bytes 5898240 | tf_op jit(solution)/shard_map/reduce_scatter | solution.py:666
  213.0 8.0 %collective-permute-start.12 = (bf16[384,192]{1,0:T(8,128)(2,1)}, bf16[384,192]{1,0:T(8,128)(2,1)S(1)}, u32[]{:S(2)}, u32[]{:S(2)}) collective-permute-start(bf16[384,192]{1,0:T(8,128)(2,1)} %get-tuple-element.81), channel_id=1, source_target_pairs={{0,16},{8,24},{16,0},{24,8},{1,17},{9,25},{17,1},{25,9},{2,18},{10... | collective-permute-start | bytes 442376 | tf_op jit(solution)/shard_map/ppermute | solution.py:30
  214.0 10.3 %collective-permute-start.13 = (bf16[384,192]{1,0:T(8,128)(2,1)}, bf16[384,192]{1,0:T(8,128)(2,1)S(1)}, u32[]{:S(2)}, u32[]{:S(2)}) collective-permute-start(bf16[384,192]{1,0:T(8,128)(2,1)} %get-tuple-element.82), channel_id=1, source_target_pairs={{0,24},{8,16},{16,8},{24,0},{1,25},{9,17},{17,9},{25,1},{2,26},{10... | collective-permute-start | bytes 442376 | tf_op jit(solution)/shard_map/ppermute | solution.py:30
  224.3 37.9 %all-to-all-start.2 = ((bf16[32,24,896]{2,1,0:T(8,128)(2,1)}), bf16[32,24,896]{2,1,0:T(8,128)(2,1)S(1)}, u32[]{:S(2)}, u32[]{:S(2)}) async-start(bf16[32,24,896]{2,1,0:T(8,128)(2,1)} %bitcast.32), calls=%async_computation.2 | async-start | bytes 2752512 | tf_op jit(solution)/shard_map/all_to_all | solution.py:703
  262.1 48.6 %all-to-all-start.3 = ((bf16[8,96,576]{2,1,0:T(8,128)(2,1)}), bf16[8,96,576]{2,1,0:T(8,128)(2,1)S(1)}, u32[]{:S(2)}, u32[]{:S(2)}) async-start(bf16[8,96,576]{2,1,0:T(8,128)(2,1)} %bitcast.33), calls=%async_computation.3 | async-start | bytes 1966080 | tf_op jit(solution)/shard_map/all_to_all | solution.py:594
  274.5 8.5 %collective-permute-start.15 = (bf16[384,768]{1,0:T(8,128)(2,1)}, bf16[384,768]{1,0:T(8,128)(2,1)S(1)}, u32[]{:S(2)}, u32[]{:S(2)}) collective-permute-start(bf16[384,768]{1,0:T(8,128)(2,1)} %get-tuple-element.101), channel_id=1, source_target_pairs={{0,8},{8,0},{16,24},{24,16},{1,9},{9,1},{17,25},{25,17},{2,10},{10... | collective-permute-start | bytes 1769480 | tf_op jit(solution)/shard_map/ppermute | solution.py:30
  282.8 17.9 %collective-permute-start.14 = (bf16[384,768]{1,0:T(8,128)(2,1)S(1)}, bf16[384,768]{1,0:T(8,128)(2,1)}, u32[]{:S(2)}, u32[]{:S(2)}) collective-permute-start(bf16[384,768]{1,0:T(8,128)(2,1)S(1)} %copy-done.13), channel_id=1, source_target_pairs={{0,8},{8,0},{16,24},{24,16},{1,9},{9,1},{17,25},{25,17},{2,10},{10... | collective-permute-start | bytes 1769480 | tf_op jit(solution)/shard_map/ppermute | solution.py:30
  283.1 17.6 %collective-permute-start.16 = (bf16[384,768]{1,0:T(8,128)(2,1)S(1)}, bf16[384,768]{1,0:T(8,128)(2,1)S(1)}, u32[]{:S(2)}, u32[]{:S(2)}) collective-permute-start(bf16[384,768]{1,0:T(8,128)(2,1)S(1)} %add_convert_fusion), channel_id=1, source_target_pairs={{0,16},{8,24},{16,0},{24,8},{1,17},{9,25},{17,1},{25,9},{2,18},{10... | collective-permute-start | bytes 1769480 | tf_op jit(solution)/shard_map/ppermute | solution.py:30
  288.3 4.5 %collective-permute-start.19 = (f32[864]{0:T(1024)S(1)}, f32[864]{0:T(1024)S(1)}, u32[]{:S(2)}, u32[]{:S(2)}) collective-permute-start(f32[864]{0:T(1024)S(1)} %add.40), channel_id=1, source_target_pairs={{0,4},{1,5},{2,6},{3,7},{4,0},{5,1},{6,2},{7,3},{8,12},{9,13},{10,... | collective-permute-start | bytes 10376 | tf_op jit(solution)/shard_map/ppermute | solution.py:30
  295.0 5.0 %collective-permute-start.21 = (f32[768]{0:T(1024)S(1)}, f32[768]{0:T(1024)S(1)}, u32[]{:S(2)}, u32[]{:S(2)}) collective-permute-start(f32[768]{0:T(1024)S(1)} %slice_add_fusion), channel_id=1, source_target_pairs={{0,16},{8,24},{16,0},{24,8},{1,17},{9,25},{17,1},{25,9},{2,18},{10... | collective-permute-start | bytes 9224 | tf_op jit(solution)/shard_map/ppermute | solution.py:30
  (30 other events, 195.5 us)
Sparse Core Ops, SparseCore 0:
  38.7 42.7 all-gather.1
  161.8 46.9 reduce-scatter.4
  211.5 60.5 reduce-scatter.2
